TPU v7x, 32 devices: a whole 2x2x4 slice. The times are simulated.
32 devices in a mesh: blk: 4 (over x, core), rows: 8 (over z, y).
Axes of the slice: x: 2, y: 2, z: 4, core: 2. Of those that a mesh axis runs over, the one named last changes fastest.
Arguments:
- fock_band: bfloat16 [8192, 2176], P('rows'), may hold values from -0.125 to 0.125
- fock_slot_mask: int32 [64, 17], P('rows'), may hold values from 0 to 1, as said below
- orbital_slab: bfloat16 [8192, 2048], P('rows', 'blk'), may hold values from -6 to 6
- orbital_mask: int32 [64, 16], P('rows', 'blk'), may hold values 0 or 1
- result_mask: int32 [64, 16], P('rows', 'blk'), may hold values 0 or 1
Outputs:
- product_slab: bfloat16 [8192, 2048], P('rows', 'blk')
- projected: float32 [2048, 2048], P('rows', 'blk')
Inputs may be any that keep to these rules, and one draw needn't show every extreme that they name: `fock_slot_mask`: 1 marks a present block slot.
All inputs are finite; a program needn't handle non-finite values. No bound on the sum of `orbital_mask` or of `result_mask` on one device may be relied on, other than what follows from the above.
Results may differ from a plain program's by a relative error of at most 0.0029.
Values may be sent and summed in bfloat16 or wider, within the bound.
A program may use at most 64 MiB of HBM per device.

v0:
```python
import math

import jax
import jax.numpy as jnp
from jax import lax
from jax.sharding import PartitionSpec as P


def with_halo(block, sides, width):
    for axis, dim in sides:
        count = lax.axis_size(axis)
        forward = [(i, i + 1) for i in range(count - 1)]
        forward.append((count - 1, 0))
        backward = [(target, source) for source, target in forward]
        low = lax.ppermute(
            lax.slice_in_dim(block, block.shape[dim] - width, None, axis=dim), axis, forward
        )
        high = lax.ppermute(lax.slice_in_dim(block, 0, width, axis=dim), axis, backward)
        block = jnp.concatenate([low, block, high], axis=dim)
    return block


def on_device(fock_band, fock_slot_mask, orbital_slab, orbital_mask, result_mask):
    local_blocks = fock_slot_mask.shape[0]
    band_extent = fock_slot_mask.shape[1]
    radius = (band_extent - 1) // 2
    block_size = fock_band.shape[0] // local_blocks
    columns = orbital_slab.shape[1]
    col_blocks = orbital_mask.shape[1]
    fock_block_list = fock_band.reshape(
        local_blocks, block_size, band_extent, block_size
    ) * fock_slot_mask[:, None, :, None].astype(jnp.bfloat16)
    slab_rows = (
        orbital_slab.reshape(local_blocks, block_size, col_blocks, block_size)
        * orbital_mask[:, None, :, None].astype(jnp.bfloat16)
    ).reshape(local_blocks * block_size, columns)
    extended = with_halo(slab_rows, (("rows", 0),), radius * block_size)
    extended = extended.reshape(local_blocks + 2 * radius, block_size, columns)

    def add_offset(band_shift, summed_total):
        band_window = lax.dynamic_slice_in_dim(extended, band_shift, local_blocks, 0)
        fock_block_piece = lax.dynamic_index_in_dim(fock_block_list, band_shift, 2, keepdims=False)
        return summed_total + jnp.einsum(
            "wnq,wqg->wng", fock_block_piece, band_window, preferred_element_type=jnp.float32
        )

    summed_total = lax.fori_loop(
        0, band_extent, add_offset, jnp.zeros((local_blocks, block_size, columns), jnp.float32)
    )
    product_slab = (
        (
            summed_total.reshape(local_blocks, block_size, col_blocks, block_size)
            * result_mask[:, None, :, None].astype(jnp.float32)
        )
        .reshape(local_blocks * block_size, columns)
        .astype(jnp.bfloat16)
    )
    groups = lax.axis_size("rows")
    factor = 1.0 / math.sqrt(local_blocks * block_size * groups)
    gathered = lax.all_gather(slab_rows, "blk", axis=1, tiled=True)
    projected = lax.psum_scatter(
        jnp.einsum("rc,rd->cd", gathered, product_slab, preferred_element_type=jnp.float32)
        * factor,
        "rows",
        scatter_dimension=0,
        tiled=True,
    )
    return (product_slab, projected)


def solution(mesh):
    placed = (
        P("rows", None),
        P("rows", None),
        P("rows", "blk"),
        P("rows", "blk"),
        P("rows", "blk"),
    )
    return jax.shard_map(
        on_device,
        mesh=mesh,
        in_specs=placed,
        out_specs=(P("rows", "blk"), P("rows", "blk")),
        check_vma=False,
    )
```

profile of v0, /device:TPU:0, one launch (start us, length us, event | category | flops | bytes accessed | tf_op | source)
XLA Modules:
  0.0 220.5 jit_solution(7946606645252785461)
XLA Ops:
  7.2 0.7 convert_element_type.16
  8.0 0.3 mul.38
  8.3 1.4 bitcast_multiply_fusion.1
  9.7 3.0 %collective-permute-start = (bf16[1024,512]{1,0:T(8,128)(2,1)S(1)}, bf16[1024,512]{1,0:T(8,128)(2,1)}, u32[]{:S(2)}, u32[]{:S(2)}) collective-permute-start(bf16[1024,512]{1,0:T(8,128)(2,1)S(1)} %bitcast_multiply_fusion.1), channel_id=1, source_target_pairs={{0,1},{1,2},{2,3},{3,4},{4,5},{5,6},{6,7},{7,0},{8,9},{9,10},{10,1... | collective-permute-start | bytes 3145736 | tf_op jit(solution)/shard_map/ppermute | solution.py:15
  12.7 3.1 %collective-permute-start.1 = (bf16[1024,512]{1,0:T(8,128)(2,1)S(1)}, bf16[1024,512]{1,0:T(8,128)(2,1)}, u32[]{:S(2)}, u32[]{:S(2)}) collective-permute-start(bf16[1024,512]{1,0:T(8,128)(2,1)S(1)} %bitcast_multiply_fusion.1), channel_id=1, source_target_pairs={{1,0},{2,1},{3,2},{4,3},{5,4},{6,5},{7,6},{0,7},{9,8},{10,9},{11,1... | collective-permute-start | bytes 3145736 | tf_op jit(solution)/shard_map/ppermute | solution.py:18
  15.9 6.5 %copy.10 = bf16[1024,2176]{0,1:T(8,128)(2,1)} copy(bf16[1024,2176]{1,0:T(8,128)(2,1)} %param.7) | data formatting | bytes 8912896 | tf_op args[0]
  22.5 6.2 %copy.16 = bf16[272,8,8,128]{3,2,1,0:T(8,128)(2,1)} copy(bf16[272,8,8,128]{3,1,2,0:T(8,128)(2,1)} %bitcast.27) | data formatting | bytes 8912896
  28.9 4.7 %broadcast_multiply_fusion = bf16[8,128,17,128]{1,0,3,2:T(8,128)(2,1)} fusion(bf16[8,128,17,128]{1,0,3,2:T(8,128)(2,1)} %bitcast.26, bf16[8,17]{0,1:T(8,128)(2,1)S(1)} %copy.11), kind=kLoop, calls=%fused_computation.7 | loop fusion | flops 2228224 | bytes 8913168 | tf_op jit(solution)/shard_map/mul | solution.py:30
  33.6 24.0 %collective-permute-done = bf16[1024,512]{1,0:T(8,128)(2,1)} collective-permute-done((bf16[1024,512]{1,0:T(8,128)(2,1)S(1)}, bf16[1024,512]{1,0:T(8,128)(2,1)}, u32[]{:S(2)}, u32[]{:S(2)}) %collective-permute-start) | collective-permute-done | bytes 1048608 | tf_op jit(solution)/shard_map/ppermute | solution.py:15
  57.6 2.3 %collective-permute-done.1 = bf16[1024,512]{1,0:T(8,128)(2,1)} collective-permute-done((bf16[1024,512]{1,0:T(8,128)(2,1)S(1)}, bf16[1024,512]{1,0:T(8,128)(2,1)}, u32[]{:S(2)}, u32[]{:S(2)}) %collective-permute-start.1) | collective-permute-done | bytes 1048608 | tf_op jit(solution)/shard_map/ppermute | solution.py:18
  59.9 3.0 %pad_maximum_fusion = bf16[3072,512]{1,0:T(8,128)(2,1)} fusion(bf16[1024,512]{1,0:T(8,128)(2,1)} %collective-permute-done.1, bf16[1024,512]{1,0:T(8,128)(2,1)S(1)} %copy-done.1, bf16[1024,512]{1,0:T(8,128)(2,1)} %collective-permute-done), kind=kLoop, calls=%fused_computation.6 | loop fusion | flops 9437184 | bytes 6291456 | tf_op jit(solution)/shard_map/concatenate | solution.py:19
  62.9 54.9 %while.14 = (s32[]{:T(128)}, f32[8,128,512]{2,1,0:T(8,128)S(1)}, bf16[8,128,17,128]{1,0,3,2:T(8,128)(2,1)}, bf16[24,128,512]{2,1,0:T(8,128)(2,1)}, s32[]{:T(128)}, /*index=5*/s32[]{:T(128)}) while((s32[]{:T(128)}, f32[8,128,512]{2,1,0:T(8,128)S(1)}, bf16[8,128,17,128]{1,0,3,2:T(8,128)(2,1)}, bf16[24,128,512]{2,1,0:T(8,128)(2,1)}, ...), condition=%wide.region_1.2_spmd.clone, body=%wide.region_0.1_spmd.clone.sunk | while | flops 135266304 | bytes 6554195 | solution.py:47
  62.9 1.0 constant_dynamic-slice_fusion.2
  63.9 0.2 copy.22
  64.1 2.0 select_add_fusion.2
  66.1 1.0 constant_dynamic-slice_fusion.2
  67.1 0.2 copy.22
  67.3 2.0 select_add_fusion.2
  69.4 1.0 constant_dynamic-slice_fusion.2
  70.3 0.2 copy.22
  70.6 2.0 select_add_fusion.2
  72.6 1.0 constant_dynamic-slice_fusion.2
  73.6 0.2 copy.22
  73.8 2.0 select_add_fusion.2
  75.8 1.0 constant_dynamic-slice_fusion.2
  76.8 0.2 copy.22
  77.0 2.0 select_add_fusion.2
  79.1 1.0 constant_dynamic-slice_fusion.2
  80.0 0.2 copy.22
  80.3 2.0 select_add_fusion.2
  82.3 1.0 constant_dynamic-slice_fusion.2
  83.3 0.2 copy.22
  83.5 2.0 select_add_fusion.2
  85.5 1.0 constant_dynamic-slice_fusion.2
  86.5 0.2 copy.22
  86.7 2.0 select_add_fusion.2
  88.7 1.0 constant_dynamic-slice_fusion.2
  89.7 0.2 copy.22
  90.0 2.0 select_add_fusion.2
  92.0 1.0 constant_dynamic-slice_fusion.2
  92.9 0.2 copy.22
  93.2 2.0 select_add_fusion.2
  95.2 1.0 constant_dynamic-slice_fusion.2
  96.2 0.2 copy.22
  96.4 2.0 select_add_fusion.2
  98.4 1.0 constant_dynamic-slice_fusion.2
  99.4 0.2 copy.22
  99.6 2.0 select_add_fusion.2
  101.7 1.0 constant_dynamic-slice_fusion.2
  102.6 0.2 copy.22
  102.9 2.0 select_add_fusion.2
  104.9 1.0 constant_dynamic-slice_fusion.2
  105.9 0.2 copy.22
  106.1 2.0 select_add_fusion.2
  108.1 1.0 constant_dynamic-slice_fusion.2
  109.3 2.0 select_add_fusion.2
  111.3 1.0 constant_dynamic-slice_fusion.2
  112.6 2.0 select_add_fusion.2
  114.6 1.0 constant_dynamic-slice_fusion.2
  115.8 2.0 select_add_fusion.2
  117.8 0.3 mul.41
  118.1 0.5 fusion.3
  118.7 6.9 %convolution_multiply_fusion = f32[2048,512]{1,0:T(8,128)} fusion(bf16[1024,2048]{1,0:T(8,128)(2,1)} %all-gather.2.cloned.1.call-done, bf16[1024,512]{1,0:T(8,128)(2,1)S(1)} %fusion.3), kind=kOutput, calls=%fused_computation.5 | convolution fusion | flops 2148532224 | bytes 9437184 | tf_op jit(solution)/shard_map/rc,rd->cd/dot_general | solution.py:62
  125.6 88.1 %reduce-scatter.2.cloned.1.call-done = f32[256,512]{1,0:T(8,128)} async-done(((f32[2048,512]{1,0:T(8,128)}), f32[256,512]{1,0:T(8,128)}) %reduce-scatter.2.cloned.1.call-update) | async-done | bytes 524304 | tf_op jit(solution)/shard_map/reduce_scatter | solution.py:61
  (24 shorter events, 1.1 us)
Async XLA Ops:
  7.2 111.5 %all-gather.2.cloned.1.call-start = ((), (), s32[]{:S(2)}) async-start(), calls=%async_computation.1 | async-start | bytes 5242880 | tf_op jit(solution)/shard_map/all_gather | solution.py:60
  9.7 6.1 %copy-start = (bf16[1024,512]{1,0:T(8,128)(2,1)}, bf16[1024,512]{1,0:T(8,128)(2,1)S(1)}, u32[]{:S(2)}) copy-start(bf16[1024,512]{1,0:T(8,128)(2,1)S(1)} %bitcast_multiply_fusion.1) | copy-start | bytes 3145732
  9.7 47.9 %collective-permute-start = (bf16[1024,512]{1,0:T(8,128)(2,1)S(1)}, bf16[1024,512]{1,0:T(8,128)(2,1)}, u32[]{:S(2)}, u32[]{:S(2)}) collective-permute-start(bf16[1024,512]{1,0:T(8,128)(2,1)S(1)} %bitcast_multiply_fusion.1), channel_id=1, source_target_pairs={{0,1},{1,2},{2,3},{3,4},{4,5},{5,6},{6,7},{7,0},{8,9},{9,10},{10,1... | collective-permute-start | bytes 3145736 | tf_op jit(solution)/shard_map/ppermute | solution.py:15
  12.7 47.2 %collective-permute-start.1 = (bf16[1024,512]{1,0:T(8,128)(2,1)S(1)}, bf16[1024,512]{1,0:T(8,128)(2,1)}, u32[]{:S(2)}, u32[]{:S(2)}) collective-permute-start(bf16[1024,512]{1,0:T(8,128)(2,1)S(1)} %bitcast_multiply_fusion.1), channel_id=1, source_target_pairs={{1,0},{2,1},{3,2},{4,3},{5,4},{6,5},{7,6},{0,7},{9,8},{10,9},{11,1... | collective-permute-start | bytes 3145736 | tf_op jit(solution)/shard_map/ppermute | solution.py:18
  15.9 197.8 %reduce-scatter.2.cloned.1.call-start = ((), (), s32[]{:S(2)}) async-start(), calls=%async_computation.2 | async-start | bytes 4718592 | tf_op jit(solution)/shard_map/reduce_scatter | solution.py:61
  22.5 6.3 %copy-start.3 = (s32[8,17]{1,0:T(8,128)S(1)}, s32[8,17]{1,0:T(8,128)}, u32[]{:S(2)}) copy-start(s32[8,17]{1,0:T(8,128)} %param.8) | copy-start | bytes 1636
  22.5 6.4 %copy-start.4 = (s32[8,4]{0,1:T(4,128)S(1)}, s32[8,4]{0,1:T(4,128)}, u32[]{:S(2)}) copy-start(s32[8,4]{0,1:T(4,128)} %param.11) | copy-start | bytes 388
  28.9 31.0 %copy-start.1 = (bf16[1024,512]{1,0:T(8,128)(2,1)S(1)}, bf16[1024,512]{1,0:T(8,128)(2,1)}, u32[]{:S(2)}) copy-start(bf16[1024,512]{1,0:T(8,128)(2,1)} %copy-done) | copy-start | bytes 3145732
  118.7 6.9 %copy-start.2 = (bf16[1024,512]{1,0:T(8,128)(2,1)}, bf16[1024,512]{1,0:T(8,128)(2,1)S(1)}, u32[]{:S(2)}) copy-start(bf16[1024,512]{1,0:T(8,128)(2,1)S(1)} %fusion.3) | copy-start | bytes 3145732
Sparse Core Ops, SparseCore 0:
  16.0 33.1 all-gather.1
  125.7 87.9 reduce-scatter.1
where the time goes:
time: 222 us; the launch traced here: 221 us
  waiting for transfers between devices  114 us (51%)
  matrix products  40.8 us (18%)
  local copies, waits for them, and re-layouts  34.1 us (15%)
  between operations  14.1 us (6%)
  other arithmetic  10.3 us (5%)
  starting transfers between devices  6.2 us (3%)
    reduce_scatter x1, waiting for transfers between devices, on_device(): lax.psum_scatter(jnp.einsum('rc,rd->cd', gathered, product_slab, preferre...  88.1 us
    dot_general x17, matrix products, add_offset(): jnp.einsum('wnq,wqg->wng', fock_block_piece, band_window, preferred_eleme...  33.9 us
    ppermute x1, waiting for transfers between devices, with_halo(): lax.ppermute(lax.slice_in_dim(block, block.shape[dim] - width, None, axis...  24 us
    dynamic_slice x34, local copies, waits for them, and re-layouts, add_offset(): lax.dynamic_index_in_dim(fock_block_list, band_shift, 2, keepdims=False)  20.4 us
    unnamed x12, local copies, waits for them, and re-layouts  12.8 us
    dot_general x1, matrix products, on_device(): jnp.einsum('rc,rd->cd', gathered, product_slab, preferred_element_type=jn...  6.88 us
    mul x1, other arithmetic, on_device(): fock_band.reshape(local_blocks, block_size, band_extent, block_size)  4.74 us
  transfers between devices with their start and end apart: 4, of which 3 were waited for; matrix products, arithmetic and copies ran while one was open for 34% of the time, Pallas kernels for 0%

commit v1 on v0

v1 whole, which is shorter than its diff:
```python
import functools
import math

import jax
import jax.numpy as jnp
from jax import lax
from jax.experimental import pallas as pl
from jax.experimental.pallas import tpu as pltpu
from jax.sharding import PartitionSpec as P

CHUNK = 256
MESH = pl.DeviceIdType.MESH


def scaled(block, flag):
    return block * jnp.full(block.shape, flag.astype(jnp.float32)).astype(block.dtype)


def kernel(
    n, nb, fmask, omask, rmask, fock_hbm, slab, prod_hbm, proj,
    fraw, fpad, ext, prod, gat, acc, send_a, recv_a, send_b, recv_b,
    near_s, near_r, far_s, far_r, x_s, x_r, c_s, c_r, f_s, f_r,
    a_s, a_r, b_s, b_r, fock_sem, prod_sem,
):
    local_blocks, band = fmask.shape
    rows, columns = slab.shape
    bs = rows // local_blocks
    chunks = columns // CHUNK
    per_chunk = CHUNK // bs
    parts = near_s.shape[1]
    part = rows // parts
    half = n // 2
    per_panel = half // nb
    csz = columns * nb // n
    pan_rows = columns // 2

    r = lax.axis_index("rows")
    b = lax.axis_index("blk")
    par = lax.rem(r, 2)
    partner = r + 1 - 2 * par
    far_to = lax.rem(r + 2 - 4 * par + n, n)
    mine = r // 2
    my_pan = mine // per_panel
    my_sub = lax.rem(mine, per_panel)
    sibling = b + 1 - 2 * lax.rem(b, 2)
    across = lax.rem(b + 2, nb)

    def remote(src, dst, ssem, rsem, rows_to=None, blk_to=None):
        return pltpu.make_async_remote_copy(
            src_ref=src, dst_ref=dst, send_sem=ssem, recv_sem=rsem,
            device_id={"rows": r if rows_to is None else rows_to, "blk": b if blk_to is None else blk_to},
            device_id_type=MESH,
        )

    barrier = pltpu.get_barrier_semaphore()
    for to in (sibling, across):
        pl.semaphore_signal(barrier, inc=1, device_id={"rows": r, "blk": to}, device_id_type=MESH)
    pl.semaphore_signal(barrier, inc=1, device_id={"rows": partner, "blk": b}, device_id_type=MESH)
    for s in range(1, half):
        pl.semaphore_signal(
            barrier, inc=1, device_id={"rows": lax.rem(r + 2 * s, n), "blk": b}, device_id_type=MESH
        )

    fock_copy = pltpu.make_async_copy(fock_hbm, fraw, fock_sem)
    fock_copy.start()

    for k in range(chunks):
        for i in range(local_blocks):
            for w in range(per_chunk):
                j = k * per_chunk + w
                ext[k, rows + i * bs : rows + (i + 1) * bs, w * bs : (w + 1) * bs] = scaled(
                    slab[i * bs : (i + 1) * bs, j * bs : (j + 1) * bs], omask[i, j]
                )

    pl.semaphore_wait(barrier, 3 + half - 1)

    def at_rows(base, q):
        return pl.ds(pl.multiple_of(base + q * part, part), part)

    near_from = 2 * rows * (1 - par)
    near_to = 2 * rows * par
    near = [
        [
            remote(
                ext.at[k, pl.ds(rows + q * part, part), :], ext.at[k, at_rows(near_to, q), :],
                near_s.at[k, q], near_r.at[k, q], rows_to=partner,
            )
            for q in range(parts)
        ]
        for k in range(chunks)
    ]
    far = [
        [
            remote(
                ext.at[k, at_rows(near_from, q), :], ext.at[k, at_rows(near_to, q), :],
                far_s.at[k, q], far_r.at[k, q], rows_to=far_to,
            )
            for q in range(parts)
        ]
        for k in range(chunks)
    ]
    for k in range(chunks):
        for q in range(parts):
            near[k][q].start()

    grain = min(csz, bs)
    for j in range(columns // bs):
        k, w = j // per_chunk, j % per_chunk
        turned = ext[k, rows : 2 * rows, w * bs : (w + 1) * bs].T
        for g in range(bs // grain):
            c = j * bs + g * grain
            t = c // csz
            at = (t // 2) * csz + c % csz
            gat[b, t % 2, at : at + grain, :] = turned[g * grain : (g + 1) * grain, :]

    order = (1 - par, par)
    over_x = [remote(gat.at[b, p], gat.at[b, p], x_s.at[u], x_r.at[u], blk_to=across) for u, p in enumerate(order)]
    to_core = [remote(gat.at[b, p], gat.at[b, p], c_s.at[u], c_r.at[u], blk_to=sibling) for u, p in enumerate(order)]
    pass_on = [
        remote(gat.at[across, p], gat.at[across, p], f_s.at[u], f_r.at[u], blk_to=sibling)
        for u, p in enumerate(order)
    ]
    for u in range(2):
        over_x[u].start()
        to_core[u].start()

    fock_copy.wait()

    def mask_pair(pair, carry):
        for h in range(2):
            at = pl.ds(pl.multiple_of((2 * pair + h) * bs, bs), bs)
            pad = 0 if h else band * bs
            fpad[at, pad : pad + bs] = jnp.zeros((bs, bs), fpad.dtype)
            for o in range(band):
                fpad[at, (o + h) * bs : (o + h + 1) * bs] = scaled(
                    fraw[at, o * bs : (o + 1) * bs], fmask[2 * pair + h, o]
                )
        return carry

    lax.fori_loop(0, local_blocks // 2, mask_pair, 0)

    def forward(k, q):
        near[k][q].wait_recv()
        far[k][q].start()

    def product(k):
        for q in range(parts):
            far[k][q].wait_recv()

        def pair_rows(pair, carry):
            at = pl.ds(pl.multiple_of(2 * pair * bs, 2 * bs), 2 * bs)
            window = pl.ds(pl.multiple_of(2 * pair * bs, 2 * bs), (band + 1) * bs)
            total = jnp.dot(fpad[at, :], ext[k, window, :], preferred_element_type=jnp.float32)
            for h in range(2):
                for w in range(per_chunk):
                    flag = rmask[2 * pair + h, k * per_chunk + w].astype(jnp.float32)
                    prod[k, pl.ds(pl.multiple_of((2 * pair + h) * bs, bs), bs), w * bs : (w + 1) * bs] = (
                        total[h * bs : (h + 1) * bs, w * bs : (w + 1) * bs] * flag
                    ).astype(prod.dtype)
            return carry

        lax.fori_loop(0, local_blocks // 2, pair_rows, 0)
        pltpu.make_async_copy(prod.at[k], prod_hbm.at[:, pl.ds(k * CHUNK, CHUNK)], prod_sem.at[k]).start()

    pans = [lax.rem(my_pan + s, nb) for s in range(1, nb + 1)]
    swap = [
        [remote(send_a.at[k, pan], recv_a.at[k, pan], a_s.at[k, s], a_r.at[k, s], rows_to=partner)
         for s, pan in enumerate(pans)]
        for k in range(chunks)
    ]

    def project_theirs(k):
        for s, pan in enumerate(pans):
            send_a[k, pan] = jnp.dot(
                gat[pan, 1 - par], prod[k], preferred_element_type=jnp.float32
            ).astype(send_a.dtype)
            swap[k][s].start()

    def project_own(k):
        for pan in pans:
            acc[k, pan] = jnp.dot(gat[pan, par], prod[k], preferred_element_type=jnp.float32)

    spread = []

    def reduce_pairs(k):
        for s, pan in enumerate(pans):
            swap[k][s].wait_recv()
            total = acc[k, pan] + recv_a[k, pan].astype(jnp.float32)
            acc[k, pan] = total
            send_b[k, pan] = total.astype(send_b.dtype)
            last = s == nb - 1
            for t in range(1 if last else 0, per_panel):
                sub = lax.rem(my_sub + t, per_panel)
                to = pan * per_panel + sub
                slot = lax.rem(mine - to + half, half) - 1
                copy = remote(
                    send_b.at[k, pan, pl.ds(pl.multiple_of(sub * csz, csz), csz), :],
                    recv_b.at[k, slot], b_s.at[k, slot], b_r.at[k, slot], rows_to=2 * to + par,
                )
                copy.start()
                spread.append(copy)

    def finish(k):
        total = acc[k, my_pan, pl.ds(pl.multiple_of(my_sub * csz, csz), csz), :]
        for slot in range(half - 1):
            remote(
                send_b.at[k, my_pan, pl.ds(0, csz), :], recv_b.at[k, slot],
                b_s.at[k, slot], b_r.at[k, slot], rows_to=partner,
            ).wait_recv()
            total = total + recv_b[k, slot].astype(jnp.float32)
        proj[:, k * CHUNK : (k + 1) * CHUNK] = total * (1.0 / math.sqrt(rows * n))

    def panels_in(u):
        over_x[u].wait_recv()
        pass_on[u].start()

    for q in range(parts):
        forward(0, q)
    panels_in(0)
    for q in range(parts - 1):
        forward(1, q)
    product(0)
    forward(1, parts - 1)
    to_core[0].wait_recv()
    pass_on[0].wait_recv()
    project_theirs(0)
    panels_in(1)
    to_core[1].wait_recv()
    pass_on[1].wait_recv()
    project_own(0)
    product(1)
    project_theirs(1)
    project_own(1)
    for k in range(chunks):
        reduce_pairs(k)
    for k in range(chunks):
        finish(k)

    for k in range(chunks):
        for q in range(parts):
            near[k][q].wait_send()
            far[k][q].wait_send()
        for s in range(nb):
            swap[k][s].wait_send()
        pltpu.make_async_copy(prod.at[k], prod_hbm.at[:, pl.ds(k * CHUNK, CHUNK)], prod_sem.at[k]).wait()
    for u in range(2):
        over_x[u].wait_send()
        to_core[u].wait_send()
        pass_on[u].wait_send()
    for copy in spread:
        copy.wait_send()


def on_device(n, nb, fock_band, fock_slot_mask, orbital_slab, orbital_mask, result_mask):
    local_blocks, band = fock_slot_mask.shape
    rows, columns = orbital_slab.shape
    bs = rows // local_blocks
    chunks = columns // CHUNK
    parts = 2
    half = n // 2
    csz = columns * nb // n
    pan_rows = columns // 2
    bf16, f32 = jnp.bfloat16, jnp.float32
    dma = pltpu.SemaphoreType.DMA
    smem = pl.BlockSpec(memory_space=pltpu.SMEM)
    vmem = pl.BlockSpec(memory_space=pltpu.VMEM)
    hbm = pl.BlockSpec(memory_space=pl.ANY)
    return pl.pallas_call(
        functools.partial(kernel, n, nb),
        out_shape=(
            jax.ShapeDtypeStruct((rows, columns), bf16),
            jax.ShapeDtypeStruct((csz, columns), f32),
        ),
        in_specs=[smem, smem, smem, hbm, vmem],
        out_specs=(hbm, vmem),
        scratch_shapes=[
            pltpu.VMEM((rows, band * bs), bf16),
            pltpu.VMEM((rows, (band + 1) * bs), bf16),
            pltpu.VMEM((chunks, 3 * rows, CHUNK), bf16),
            pltpu.VMEM((chunks, rows, CHUNK), bf16),
            pltpu.VMEM((nb, 2, pan_rows, rows), bf16),
            pltpu.VMEM((chunks, nb, pan_rows, CHUNK), f32),
            pltpu.VMEM((chunks, nb, pan_rows, CHUNK), bf16),
            pltpu.VMEM((chunks, nb, pan_rows, CHUNK), bf16),
            pltpu.VMEM((chunks, nb, pan_rows, CHUNK), bf16),
            pltpu.VMEM((chunks, half - 1, csz, CHUNK), bf16),
            dma((chunks, parts)), dma((chunks, parts)), dma((chunks, parts)), dma((chunks, parts)),
            dma((2,)), dma((2,)), dma((2,)), dma((2,)), dma((2,)), dma((2,)),
            dma((chunks, nb)), dma((chunks, nb)),
            dma((chunks, half - 1)), dma((chunks, half - 1)),
            dma(()), dma((chunks,)),
        ],
        compiler_params=pltpu.CompilerParams(
            collective_id=0, has_side_effects=True, vmem_limit_bytes=50 * 1024 * 1024
        ),
        cost_estimate=pl.CostEstimate(
            flops=2 * rows * columns * (band * bs + columns * nb), bytes_accessed=8 * 2**20, transcendentals=0
        ),
    )(fock_slot_mask, orbital_mask, result_mask, fock_band, orbital_slab)


def solution(mesh):
    placed = (
        P("rows", None),
        P("rows", None),
        P("rows", "blk"),
        P("rows", "blk"),
        P("rows", "blk"),
    )
    return jax.shard_map(
        functools.partial(on_device, mesh.shape["rows"], mesh.shape["blk"]),
        mesh=mesh,
        in_specs=placed,
        out_specs=(P("rows", "blk"), P("rows", "blk")),
        check_vma=False,
    )
```

time: 222 us -> 68.3 us (0.31)
  waiting for transfers between devices: 114 us -> 0 us
  Pallas kernels: 0 us -> 61.8 us
  matrix products: 40.8 us -> 0 us
  local copies, waits for them, and re-layouts: 34.1 us -> 5.19 us
  between operations: 14.1 us -> 0.64 us
  other arithmetic: 10.3 us -> 0 us
  starting transfers between devices: 6.2 us -> 0 us
    reduce_scatter x1 -> x0, waiting for transfers between devices: 88.1 us -> none  [on_device(): lax.psum_scatter(jnp.einsum('rc,rd->cd', gathered, product_slab, preferre...]
    pallas_call x0 -> x1, Pallas kernels: none -> 61.8 us  [on_device(): pl.pallas_call(functools.partial(kernel, n, nb), out_shape=(jax.ShapeDtyp...]
    dot_general x18 -> x0, matrix products: 40.8 us -> none  [the longest x17 33.9 us: add_offset(): jnp.einsum('wnq,wqg->wng', fock_block_piece, band_window, preferred_eleme...]
    ppermute x2 -> x0, waiting for transfers between devices: 26.3 us -> none  [the longest x1 24 us: with_halo(): lax.ppermute(lax.slice_in_dim(block, block.shape[dim] - width, None, axis...]
    dynamic_slice x34 -> x0, local copies, waits for them, and re-layouts: 20.4 us -> none  [add_offset(): lax.dynamic_index_in_dim(fock_block_list, band_shift, 2, keepdims=False)]
    unnamed x12 -> x8, local copies, waits for them, and re-layouts: 12.8 us -> 5.19 us
    ppermute x2 -> x0, starting transfers between devices: 6.12 us -> none  [the longest x1 3.1 us: with_halo(): lax.ppermute(lax.slice_in_dim(block, 0, width, axis=dim), axis, backward)]
    mul x2 -> x0, other arithmetic: 6.11 us -> none  [the longest x1 4.74 us: on_device(): fock_band.reshape(local_blocks, block_size, band_extent, block_size)]
  transfers between devices with their start and end apart: 4 -> 0, of which waited for: 3 -> 0; matrix products, arithmetic and copies ran while one was open for 34% -> 0% of each run, Pallas kernels for 0% -> 0%
where the time goes in v1:
time: 68.3 us; the launch traced here: 67.6 us
  Pallas kernels  61.8 us (90%)
  local copies, waits for them, and re-layouts  5.19 us (8%)
    pallas_call x1, Pallas kernels, on_device(): pl.pallas_call(functools.partial(kernel, n, nb), out_shape=(jax.ShapeDtyp...  61.8 us
    unnamed x8, local copies, waits for them, and re-layouts  5.19 us

profile of v1, /device:TPU:0, one launch (start us, length us, event | category | flops | bytes accessed | tf_op | source)
XLA Modules:
  0.0 67.6 jit_solution(6126343160490741791)
XLA Ops:
  0.6 0.8 %copy.7.omask = s32[8,4]{1,0:T(8,128)S(1)} copy(s32[8,4]{0,1:T(4,128)} %param.8) | data formatting | bytes 256 | tf_op args[3]
  1.4 0.8 %copy.8.rmask = s32[8,4]{1,0:T(8,128)S(1)} copy(s32[8,4]{0,1:T(4,128)} %param.9) | data formatting | bytes 256 | tf_op args[4]
  2.1 0.0 copy-start
  2.1 1.2 %copy-done = bf16[1024,512]{1,0:T(8,128)(2,1)S(1)} copy-done((bf16[1024,512]{1,0:T(8,128)(2,1)S(1)}, bf16[1024,512]{1,0:T(8,128)(2,1)}, u32[]{:S(2)}) %copy-start) | copy-done | bytes 1048600
  3.4 0.0 copy-start.1
  3.4 0.7 %copy-done.1 = s32[8,17]{1,0:T(8,128)S(1)} copy-done((s32[8,17]{1,0:T(8,128)S(1)}, s32[8,17]{1,0:T(8,128)}, u32[]{:S(2)}) %copy-start.1) | copy-done | bytes 568
  4.1 61.8 %shard_map.68 = (bf16[1024,512]{1,0:T(8,128)(2,1)S(1)}, f32[256,512]{1,0:T(8,128)S(1)}) custom-call(s32[8,17]{1,0:T(8,128)S(1)} %copy-done.1, s32[8,4]{1,0:T(8,128)S(1)} %copy.7.omask, s32[8,4]{1,0:T(8,128)S(1)} %copy.8.rmask, bf16[1024,2176]{1,0:T(8,128)(2,1)} %fock_hbm.1, bf16[1024,512]{1,0:T(8,128)(2,1)S(1)} %copy-done), custom_call_target="tpu_custom_call" | custom-call | flops 4429185024 | bytes 8388608 | tf_op jit(solution)/shard_map/pallas_call | solution.py:268
  65.9 1.0 %copy.11 = bf16[1024,512]{1,0:T(8,128)(2,1)} copy(bf16[1024,512]{1,0:T(8,128)(2,1)S(1)} %get-tuple-element.4) | data formatting | bytes 2097152
  66.8 0.8 %copy.12 = f32[256,512]{1,0:T(8,128)} copy(f32[256,512]{1,0:T(8,128)S(1)} %get-tuple-element.5) | data formatting | bytes 1048576
Async XLA Ops:
  2.1 1.2 %copy-start = (bf16[1024,512]{1,0:T(8,128)(2,1)S(1)}, bf16[1024,512]{1,0:T(8,128)(2,1)}, u32[]{:S(2)}) copy-start(bf16[1024,512]{1,0:T(8,128)(2,1)} %slab.1) | copy-start | bytes 3145732
  3.4 0.7 %copy-start.1 = (s32[8,17]{1,0:T(8,128)S(1)}, s32[8,17]{1,0:T(8,128)}, u32[]{:S(2)}) copy-start(s32[8,17]{1,0:T(8,128)} %fmask.1) | copy-start | bytes 1636

commit v2 on v1

v2 whole, which is shorter than its diff:
```python
import functools
import math

import jax
import jax.numpy as jnp
from jax import lax
from jax.experimental import pallas as pl
from jax.experimental.pallas import tpu as pltpu
from jax.sharding import PartitionSpec as P

CHUNK = 256
MESH = pl.DeviceIdType.MESH


def scaled(block, flag):
    return block * jnp.full(block.shape, flag.astype(jnp.float32)).astype(block.dtype)


def kernel(
    n, nb, fmask_hbm, omask_hbm, rmask_hbm, fock_hbm, slab_hbm, prod_hbm, proj,
    fmask, omask, rmask, slab, fraw, fpad, ext, prod, gat, acc,
    send_a, recv_a, send_b, recv_b, send_c, recv_c,
    near_s, near_r, far_s, far_r, x_s, x_r, c_s, c_r, f_s, f_r,
    a_s, a_r, b_s, b_r, d_s, d_r, fock_sem, mask_sem, slab_sem, prod_sem,
):
    local_blocks, band = fmask_hbm.shape
    rows, columns = slab_hbm.shape
    bs = rows // local_blocks
    chunks = columns // CHUNK
    per_chunk = CHUNK // bs
    parts = near_s.shape[1]
    part = rows // parts
    quarter = n // 4
    csz = columns * nb // n
    groups, brows, gsubs = acc.shape[2], acc.shape[3], acc.shape[3] // csz

    r = lax.axis_index("rows")
    b = lax.axis_index("blk")
    par = lax.rem(r, 2)
    bit = lax.rem(r // 2, 2)
    rest = r // 4
    partner = r + 1 - 2 * par
    second = r + 2 - 4 * bit
    far_to = lax.rem(r + 2 - 4 * par + n, n)
    far_from = lax.rem(r - 2 + 4 * par + n, n)
    my_group = rest // gsubs
    my_sub = lax.rem(rest, gsubs)
    sibling = b + 1 - 2 * lax.rem(b, 2)
    across = lax.rem(b + 2, nb)

    def remote(src, dst, ssem, rsem, rows_to=None, blk_to=None):
        return pltpu.make_async_remote_copy(
            src_ref=src, dst_ref=dst, send_sem=ssem, recv_sem=rsem,
            device_id={"rows": r if rows_to is None else rows_to, "blk": b if blk_to is None else blk_to},
            device_id_type=MESH,
        )

    barrier = pltpu.get_barrier_semaphore()
    for to in (sibling, across):
        pl.semaphore_signal(barrier, inc=1, device_id={"rows": r, "blk": to}, device_id_type=MESH)
    peers = [partner, far_to, far_from] + [lax.rem(r + 4 * s, n) for s in range(1, quarter)]
    for to in peers:
        pl.semaphore_signal(barrier, inc=1, device_id={"rows": to, "blk": b}, device_id_type=MESH)

    slab_copies = [
        pltpu.make_async_copy(slab_hbm.at[:, pl.ds(k * CHUNK, CHUNK)], slab.at[k], slab_sem.at[k])
        for k in range(chunks)
    ]
    mask_copies = [
        pltpu.make_async_copy(src, dst, mask_sem.at[m])
        for m, (src, dst) in enumerate(((omask_hbm, omask), (fmask_hbm, fmask), (rmask_hbm, rmask)))
    ]
    fock_copy = pltpu.make_async_copy(fock_hbm, fraw, fock_sem)
    for copy in [mask_copies[0]] + slab_copies + mask_copies[1:] + [fock_copy]:
        copy.start()
    mask_copies[0].wait()

    def mask_chunk(k):
        slab_copies[k].wait()
        for i in range(local_blocks):
            for w in range(per_chunk):
                ext[k, rows + i * bs : rows + (i + 1) * bs, w * bs : (w + 1) * bs] = scaled(
                    slab[k, i * bs : (i + 1) * bs, w * bs : (w + 1) * bs], omask[k * per_chunk + w, i]
                )

    mask_chunk(0)
    pl.semaphore_wait(barrier, 2 + len(peers))

    def at_rows(base, q):
        return pl.ds(pl.multiple_of(base + q * part, part), part)

    near_from = 2 * rows * (1 - par)
    near_to = 2 * rows * par
    near = [
        [
            remote(
                ext.at[k, pl.ds(rows + q * part, part), :], ext.at[k, at_rows(near_to, q), :],
                near_s.at[k, q], near_r.at[k, q], rows_to=partner,
            )
            for q in range(parts)
        ]
        for k in range(chunks)
    ]
    far = [
        [
            remote(
                ext.at[k, at_rows(near_from, q), :], ext.at[k, at_rows(near_to, q), :],
                far_s.at[k, q], far_r.at[k, q], rows_to=far_to,
            )
            for q in range(parts)
        ]
        for k in range(chunks)
    ]
    for k in range(chunks):
        if k:
            mask_chunk(k)
        for q in range(parts):
            near[k][q].start()

    grain = min(csz, bs)
    for j in range(columns // bs):
        k, w = j // per_chunk, j % per_chunk
        turned = ext[k, rows : 2 * rows, w * bs : (w + 1) * bs].T
        for g in range(bs // grain):
            c = j * bs + g * grain
            t = c // csz
            at = (t // 2 % 2) * brows + (t // 4) * csz + c % csz
            gat[b, t % 2, at : at + grain, :] = turned[g * grain : (g + 1) * grain, :]

    order = (1 - par, par)
    over_x = [remote(gat.at[b, p], gat.at[b, p], x_s.at[u], x_r.at[u], blk_to=across) for u, p in enumerate(order)]
    to_core = [remote(gat.at[b, p], gat.at[b, p], c_s.at[u], c_r.at[u], blk_to=sibling) for u, p in enumerate(order)]
    pass_on = [
        remote(gat.at[across, p], gat.at[across, p], f_s.at[u], f_r.at[u], blk_to=sibling)
        for u, p in enumerate(order)
    ]
    for u in range(2):
        over_x[u].start()
        to_core[u].start()

    for copy in mask_copies[1:] + [fock_copy]:
        copy.wait()

    def mask_pair(pair, carry):
        for h in range(2):
            at = pl.ds(pl.multiple_of((2 * pair + h) * bs, bs), bs)
            pad = 0 if h else band * bs
            fpad[at, pad : pad + bs] = jnp.zeros((bs, bs), fpad.dtype)
            for o in range(band):
                fpad[at, (o + h) * bs : (o + h + 1) * bs] = scaled(
                    fraw[at, o * bs : (o + 1) * bs], fmask[2 * pair + h, o]
                )
        return carry

    lax.fori_loop(0, local_blocks // 2, mask_pair, 0)

    def forward(k, q):
        near[k][q].wait_recv()
        far[k][q].start()

    def product(k):
        for q in range(parts):
            far[k][q].wait_recv()

        def pair_rows(pair, carry):
            at = pl.ds(pl.multiple_of(2 * pair * bs, 2 * bs), 2 * bs)
            window = pl.ds(pl.multiple_of(2 * pair * bs, 2 * bs), (band + 1) * bs)
            total = jnp.dot(fpad[at, :], ext[k, window, :], preferred_element_type=jnp.float32)
            for h in range(2):
                for w in range(per_chunk):
                    flag = rmask[k * per_chunk + w, 2 * pair + h].astype(jnp.float32)
                    prod[k, pl.ds(pl.multiple_of((2 * pair + h) * bs, bs), bs), w * bs : (w + 1) * bs] = (
                        total[h * bs : (h + 1) * bs, w * bs : (w + 1) * bs] * flag
                    ).astype(prod.dtype)
            return carry

        lax.fori_loop(0, local_blocks // 2, pair_rows, 0)
        pltpu.make_async_copy(prod.at[k], prod_hbm.at[:, pl.ds(k * CHUNK, CHUNK)], prod_sem.at[k]).start()

    order_g = [lax.rem(my_group + s, groups) for s in range(1, groups + 1)]
    blocks = [(other, s, bit + other * (1 - 2 * bit), g) for other in (1, 0) for s, g in enumerate(order_g)]

    def panel_rows(p, q, g):
        if brows == gat.shape[2]:
            return gat[2 * g + q, p]
        return gat[g, p, pl.ds(pl.multiple_of(q * brows, brows), brows), :]

    swap = [
        [remote(send_a.at[k, q, g], recv_a.at[k, q, g], a_s.at[k, x], a_r.at[k, x], rows_to=partner)
         for x, (_, _, q, g) in enumerate(blocks)]
        for k in range(chunks)
    ]
    pairs = [
        [remote(send_b.at[k, g], recv_b.at[k, g], b_s.at[k, s], b_r.at[k, s], rows_to=second)
         for s, g in enumerate(order_g)]
        for k in range(chunks)
    ]

    def project_theirs(k):
        for x, (_, _, q, g) in enumerate(blocks):
            send_a[k, q, g] = jnp.dot(
                panel_rows(1 - par, q, g), prod[k], preferred_element_type=jnp.float32
            ).astype(send_a.dtype)
            swap[k][x].start()

    def project_own(k):
        for _, _, q, g in blocks:
            acc[k, q, g] = jnp.dot(panel_rows(par, q, g), prod[k], preferred_element_type=jnp.float32)

    spread = []

    def reduce(k, x):
        other, s, q, g = blocks[x]
        swap[k][x].wait_recv()
        total = acc[k, q, g] + recv_a[k, q, g].astype(jnp.float32)
        if other:
            send_b[k, g] = total.astype(send_b.dtype)
            pairs[k][s].start()
            return
        pairs[k][s].wait_recv()
        total = total + recv_b[k, g].astype(jnp.float32)
        last = s == groups - 1
        if last:
            acc[k, q, g] = total
        if last and gsubs == 1:
            return
        send_c[k, g] = total.astype(send_c.dtype)
        for t in range(1 if last else 0, gsubs):
            sub = lax.rem(my_sub + t, gsubs)
            to = g * gsubs + sub
            slot = lax.rem(rest - to + quarter, quarter) - 1
            copy = remote(
                send_c.at[k, g, pl.ds(pl.multiple_of(sub * csz, csz), csz), :],
                recv_c.at[k, slot], d_s.at[k, slot], d_r.at[k, slot], rows_to=4 * to + 2 * bit + par,
            )
            copy.start()
            spread.append(copy)

    def finish(k):
        total = acc[k, bit, my_group, pl.ds(pl.multiple_of(my_sub * csz, csz), csz), :]
        for slot in range(quarter - 1):
            remote(
                send_c.at[k, my_group, pl.ds(0, csz), :], recv_c.at[k, slot],
                d_s.at[k, slot], d_r.at[k, slot], rows_to=partner,
            ).wait_recv()
            total = total + recv_c[k, slot].astype(jnp.float32)
        proj[:, k * CHUNK : (k + 1) * CHUNK] = total * (1.0 / math.sqrt(rows * n))

    def panels_in(u):
        over_x[u].wait_recv()
        pass_on[u].start()

    for q in range(parts):
        forward(0, q)
    panels_in(0)
    for q in range(parts - 1):
        forward(1, q)
    product(0)
    to_core[0].wait_recv()
    pass_on[0].wait_recv()
    project_theirs(0)
    forward(1, parts - 1)
    panels_in(1)
    to_core[1].wait_recv()
    pass_on[1].wait_recv()
    project_own(0)
    for x in range(groups):
        reduce(0, x)
    product(1)
    project_theirs(1)
    for x in range(groups, 2 * groups):
        reduce(0, x)
    project_own(1)
    for x in range(groups):
        reduce(1, x)
    finish(0)
    for x in range(groups, 2 * groups):
        reduce(1, x)
    finish(1)

    for k in range(chunks):
        for q in range(parts):
            near[k][q].wait_send()
            far[k][q].wait_send()
        for copy in swap[k] + pairs[k]:
            copy.wait_send()
        pltpu.make_async_copy(prod.at[k], prod_hbm.at[:, pl.ds(k * CHUNK, CHUNK)], prod_sem.at[k]).wait()
    for u in range(2):
        over_x[u].wait_send()
        to_core[u].wait_send()
        pass_on[u].wait_send()
    for copy in spread:
        copy.wait_send()


def on_device(n, nb, fock_band, fock_slot_mask, orbital_slab, orbital_mask, result_mask):
    local_blocks, band = fock_slot_mask.shape
    rows, columns = orbital_slab.shape
    bs = rows // local_blocks
    chunks = columns // CHUNK
    parts = 2
    quarter = n // 4
    csz = columns * nb // n
    pan_rows = columns // 2
    groups, brows = (nb // 2, pan_rows) if n == 2 * nb else (nb, pan_rows // 2)
    bf16, f32 = jnp.bfloat16, jnp.float32
    dma = pltpu.SemaphoreType.DMA
    vmem = pl.BlockSpec(memory_space=pltpu.VMEM)
    hbm = pl.BlockSpec(memory_space=pltpu.HBM)
    return pl.pallas_call(
        functools.partial(kernel, n, nb),
        out_shape=(
            jax.ShapeDtypeStruct((rows, columns), bf16),
            jax.ShapeDtypeStruct((csz, columns), f32),
        ),
        in_specs=[hbm] * 5,
        out_specs=(pl.BlockSpec(memory_space=pl.ANY), vmem),
        scratch_shapes=[
            pltpu.SMEM(fock_slot_mask.shape, jnp.int32),
            pltpu.SMEM(orbital_mask.shape[::-1], jnp.int32),
            pltpu.SMEM(result_mask.shape[::-1], jnp.int32),
            pltpu.VMEM((chunks, rows, CHUNK), bf16),
            pltpu.VMEM((rows, band * bs), bf16),
            pltpu.VMEM((rows, (band + 1) * bs), bf16),
            pltpu.VMEM((chunks, 3 * rows, CHUNK), bf16),
            pltpu.VMEM((chunks, rows, CHUNK), bf16),
            pltpu.VMEM((nb, 2, pan_rows, rows), bf16),
            pltpu.VMEM((chunks, 2, groups, brows, CHUNK), f32),
            pltpu.VMEM((chunks, 2, groups, brows, CHUNK), bf16),
            pltpu.VMEM((chunks, 2, groups, brows, CHUNK), bf16),
            pltpu.VMEM((chunks, groups, brows, CHUNK), bf16),
            pltpu.VMEM((chunks, groups, brows, CHUNK), bf16),
            pltpu.VMEM((chunks, groups, brows, CHUNK), bf16),
            pltpu.VMEM((chunks, quarter - 1, csz, CHUNK), bf16),
            dma((chunks, parts)), dma((chunks, parts)), dma((chunks, parts)), dma((chunks, parts)),
            dma((2,)), dma((2,)), dma((2,)), dma((2,)), dma((2,)), dma((2,)),
            dma((chunks, 2 * groups)), dma((chunks, 2 * groups)),
            dma((chunks, groups)), dma((chunks, groups)),
            dma((chunks, quarter - 1)), dma((chunks, quarter - 1)),
            dma(()), dma((3,)), dma((chunks,)), dma((chunks,)),
        ],
        compiler_params=pltpu.CompilerParams(
            collective_id=0, has_side_effects=True, vmem_limit_bytes=64 * 2**20 - 2**17
        ),
        cost_estimate=pl.CostEstimate(
            flops=2 * rows * columns * (band * bs + columns * nb), bytes_accessed=8 * 2**20, transcendentals=0
        ),
    )(fock_slot_mask, orbital_mask.T, result_mask.T, fock_band, orbital_slab)


def solution(mesh):
    placed = (
        P("rows", None),
        P("rows", None),
        P("rows", "blk"),
        P("rows", "blk"),
        P("rows", "blk"),
    )
    return jax.shard_map(
        functools.partial(on_device, mesh.shape["rows"], mesh.shape["blk"]),
        mesh=mesh,
        in_specs=placed,
        out_specs=(P("rows", "blk"), P("rows", "blk")),
        check_vma=False,
    )
```

time: 68.3 us -> 61.7 us (0.903)
  Pallas kernels: 61.8 us -> 56.7 us
  local copies, waits for them, and re-layouts: 5.19 us -> 4.13 us
    pallas_call x1, Pallas kernels: 61.8 us -> 56.7 us  [on_device(): pl.pallas_call(functools.partial(kernel, n, nb), out_shape=(jax.ShapeDtyp...]
    unnamed x8 -> x2, local copies, waits for them, and re-layouts: 5.19 us -> 4.13 us
where the time goes in v2:
time: 61.7 us; the launch traced here: 61.5 us
  Pallas kernels  56.7 us (92%)
  local copies, waits for them, and re-layouts  4.13 us (7%)
  between operations  0.64 us (1%)
    pallas_call x1, Pallas kernels, on_device(): pl.pallas_call(functools.partial(kernel, n, nb), out_shape=(jax.ShapeDtyp...  56.7 us
    unnamed x2, local copies, waits for them, and re-layouts  4.13 us

profile of v2, /device:TPU:0, one launch (start us, length us, event | category | flops | bytes accessed | tf_op | source)
XLA Modules:
  0.0 61.5 jit_solution(843168146136968198)
XLA Ops:
  0.6 56.7 %shard_map.68 = (bf16[1024,512]{1,0:T(8,128)(2,1)}, f32[256,512]{1,0:T(8,128)}) custom-call(s32[8,17]{1,0:T(8,128)} %fmask_hbm.1, s32[4,8]{1,0:T(4,128)} %bitcast.2, s32[4,8]{1,0:T(4,128)} %bitcast.3, bf16[1024,2176]{1,0:T(8,128)(2,1)} %fock_hbm.1, bf16[1024,512]{1,0:T(8,128)(2,1)} %slab_hbm.1), custom_call_target="tpu_custom_call" | custom-call | flops 4429185024 | bytes 8388608 | tf_op jit(solution)/shard_map/pallas_call | solution.py:310
  57.4 2.3 %copy.9 = bf16[1024,512]{1,0:T(8,128)(2,1)} copy(bf16[1024,512]{1,0:T(8,128)(2,1)} %get-tuple-element.4) | data formatting | bytes 2097152
  59.7 1.9 %copy.10 = f32[256,512]{1,0:T(8,128)} copy(f32[256,512]{1,0:T(8,128)} %get-tuple-element.5) | data formatting | bytes 1048576

commit v3 on v2

--- a/solution.py
+++ b/solution.py
@@ -253,13 +253,14 @@
     for q in range(parts):
         forward(0, q)
     panels_in(0)
-    for q in range(parts - 1):
-        forward(1, q)
+    forward(1, 0)
     product(0)
+    forward(1, 1)
     to_core[0].wait_recv()
     pass_on[0].wait_recv()
     project_theirs(0)
-    forward(1, parts - 1)
+    for q in range(2, parts):
+        forward(1, q)
     panels_in(1)
     to_core[1].wait_recv()
     pass_on[1].wait_recv()
@@ -298,7 +299,7 @@
     rows, columns = orbital_slab.shape
     bs = rows // local_blocks
     chunks = columns // CHUNK
-    parts = 2
+    parts = 4
     quarter = n // 4
     csz = columns * nb // n
     pan_rows = columns // 2
@@ -340,7 +341,7 @@
             dma(()), dma((3,)), dma((chunks,)), dma((chunks,)),
         ],
         compiler_params=pltpu.CompilerParams(
-            collective_id=0, has_side_effects=True, vmem_limit_bytes=64 * 2**20 - 2**17
+            collective_id=0, has_side_effects=True, vmem_limit_bytes=62 * 2**20
         ),
         cost_estimate=pl.CostEstimate(
             flops=2 * rows * columns * (band * bs + columns * nb), bytes_accessed=8 * 2**20, transcendentals=0

time: 61.7 us -> 62.3 us (level)
  Pallas kernels: 56.7 us -> 57.4 us
    pallas_call x1, Pallas kernels: 56.7 us -> 57.4 us  [on_device(): pl.pallas_call(functools.partial(kernel, n, nb), out_shape=(jax.ShapeDtyp...]
where the time goes in v3:
time: 62.3 us; the launch traced here: 62.1 us
  Pallas kernels  57.4 us (92%)
  local copies, waits for them, and re-layouts  4.13 us (7%)
  between operations  0.64 us (1%)
    pallas_call x1, Pallas kernels, on_device(): pl.pallas_call(functools.partial(kernel, n, nb), out_shape=(jax.ShapeDtyp...  57.4 us
    unnamed x2, local copies, waits for them, and re-layouts  4.13 us

profile of v3, /device:TPU:0, one launch (start us, length us, event | category | flops | bytes accessed | tf_op | source)
XLA Modules:
  0.0 62.1 jit_solution(7021561732862862993)
XLA Ops:
  0.6 57.4 %shard_map.68 = (bf16[1024,512]{1,0:T(8,128)(2,1)}, f32[256,512]{1,0:T(8,128)}) custom-call(s32[8,17]{1,0:T(8,128)} %fmask_hbm.1, s32[4,8]{1,0:T(4,128)} %bitcast.2, s32[4,8]{1,0:T(4,128)} %bitcast.3, bf16[1024,2176]{1,0:T(8,128)(2,1)} %fock_hbm.1, bf16[1024,512]{1,0:T(8,128)(2,1)} %slab_hbm.1), custom_call_target="tpu_custom_call" | custom-call | flops 4429185024 | bytes 8388608 | tf_op jit(solution)/shard_map/pallas_call | solution.py:311
  58.0 2.3 %copy.9 = bf16[1024,512]{1,0:T(8,128)(2,1)} copy(bf16[1024,512]{1,0:T(8,128)(2,1)} %get-tuple-element.4) | data formatting | bytes 2097152
  60.3 1.9 %copy.10 = f32[256,512]{1,0:T(8,128)} copy(f32[256,512]{1,0:T(8,128)} %get-tuple-element.5) | data formatting | bytes 1048576

commit v4 on v3

--- a/solution.py
+++ b/solution.py
@@ -244,7 +244,7 @@
                 d_s.at[k, slot], d_r.at[k, slot], rows_to=partner,
             ).wait_recv()
             total = total + recv_c[k, slot].astype(jnp.float32)
-        proj[:, k * CHUNK : (k + 1) * CHUNK] = total * (1.0 / math.sqrt(rows * n))
+        proj[:, k * CHUNK : (k + 1) * CHUNK] = total
 
     def panels_in(u):
         over_x[u].wait_recv()
@@ -308,7 +308,7 @@
     dma = pltpu.SemaphoreType.DMA
     vmem = pl.BlockSpec(memory_space=pltpu.VMEM)
     hbm = pl.BlockSpec(memory_space=pltpu.HBM)
-    return pl.pallas_call(
+    product_slab, terms = pl.pallas_call(
         functools.partial(kernel, n, nb),
         out_shape=(
             jax.ShapeDtypeStruct((rows, columns), bf16),
@@ -347,6 +347,7 @@
             flops=2 * rows * columns * (band * bs + columns * nb), bytes_accessed=8 * 2**20, transcendentals=0
         ),
     )(fock_slot_mask, orbital_mask.T, result_mask.T, fock_band, orbital_slab)
+    return product_slab, terms * (1.0 / math.sqrt(rows * n))
 
 
 def solution(mesh):

time: 62.3 us -> 62.4 us (level)
  other arithmetic: 0 us -> 1.89 us
  local copies, waits for them, and re-layouts: 4.13 us -> 2.26 us
    mul x0 -> x1, other arithmetic: none -> 1.89 us  [on_device(): return (product_slab, terms * (1.0 / math.sqrt(rows * n)))]
    unnamed x2 -> x1, local copies, waits for them, and re-layouts: 4.13 us -> 2.26 us
where the time goes in v4:
time: 62.4 us; the launch traced here: 62.2 us
  Pallas kernels  57.4 us (92%)
  local copies, waits for them, and re-layouts  2.26 us (4%)
  other arithmetic  1.89 us (3%)
  between operations  0.64 us (1%)
    pallas_call x1, Pallas kernels, on_device(): pl.pallas_call(functools.partial(kernel, n, nb), out_shape=(jax.ShapeDtyp...  57.4 us
    unnamed x1, local copies, waits for them, and re-layouts  2.26 us
    mul x1, other arithmetic, on_device(): return (product_slab, terms * (1.0 / math.sqrt(rows * n)))  1.89 us

profile of v4, /device:TPU:0, one launch (start us, length us, event | category | flops | bytes accessed | tf_op | source)
XLA Modules:
  0.0 62.2 jit_solution(11438137413591734880)
XLA Ops:
  0.6 57.4 %shard_map.68 = (bf16[1024,512]{1,0:T(8,128)(2,1)}, f32[256,512]{1,0:T(8,128)}) custom-call(s32[8,17]{1,0:T(8,128)} %fmask_hbm.1, s32[4,8]{1,0:T(4,128)} %bitcast.2, s32[4,8]{1,0:T(4,128)} %bitcast.3, bf16[1024,2176]{1,0:T(8,128)(2,1)} %fock_hbm.1, bf16[1024,512]{1,0:T(8,128)(2,1)} %slab_hbm.1), custom_call_target="tpu_custom_call" | custom-call | flops 4429185024 | bytes 8388608 | tf_op jit(solution)/shard_map/pallas_call | solution.py:311
  58.0 1.9 %broadcast_multiply_fusion = f32[256,512]{1,0:T(8,128)} fusion(f32[256,512]{1,0:T(8,128)} %get-tuple-element.5), kind=kLoop, calls=%fused_computation | loop fusion | flops 131072 | bytes 1048576 | tf_op jit(solution)/shard_map/mul | solution.py:350
  59.9 2.3 %copy.8 = bf16[1024,512]{1,0:T(8,128)(2,1)} copy(bf16[1024,512]{1,0:T(8,128)(2,1)} %get-tuple-element.8) | data formatting | bytes 2097152
